TPU v7x, 32 devices: a whole 2x2x4 slice. The times are simulated.
32 devices in a mesh: row: 8 (over y, x, core), col: 4 (over z).
Axes of the slice: x: 2, y: 2, z: 4, core: 2. Of those that a mesh axis runs over, the one named last changes fastest.
Arguments:
- edge_tensor: float32 [1024, 16, 1024], P('row'), may hold values from -0.0234375 to 0.0234375
- site_tensor: float32 [16, 16, 16, 16], replicated, may hold values from -0.375 to 0.375
- left_isometry: float32 [1024, 16, 1024], P('row'), may hold values from -0.0234375 to 0.0234375
- right_isometry: float32 [512, 16, 1024], P('col', None, 'row'), may hold values from -0.03125 to 0.03125
- cotangent: float32 [512, 16, 1024], P('col', None, 'row'), may hold values from -96 to 96
Outputs:
- edge_gradient: float32 [1024, 16, 1024], P('row', 'col')
- site_gradient: float32 [16, 16, 16, 16], replicated
- left_gradient: float32 [1024, 16, 1024], P('row', 'col')
- right_gradient: float32 [512, 16, 1024], P('col', 'row')
All inputs are finite; a program needn't handle non-finite values.
Results may differ from a plain program's by a relative error of at most 0.0003.
Values sent between devices are 32-bit elements; how exact they have to be, the bound alone decides.
A program may use at most 192 MiB of HBM per device.

v0:
```python
import jax
import jax.numpy as jnp
from jax import lax
from jax.sharding import PartitionSpec as P


def on_device(edge_tensor, site_tensor, left_isometry, right_isometry, cotangent):
    highest = lax.Precision.HIGHEST
    block_rows = edge_tensor.shape[0]
    bond_width = site_tensor.shape[0]
    local_cols = right_isometry.shape[0]
    square = bond_width * bond_width
    site_matrix = jnp.transpose(site_tensor, (1, 2, 0, 3)).reshape(square, square)
    right_whole = lax.all_gather(right_isometry, "row", axis=2, tiled=True)
    first_section = jnp.einsum("aeb,cfb->acef", edge_tensor, right_whole, precision=highest)
    first_flat = first_section.reshape(block_rows, local_cols, square)
    second_flat = jnp.dot(first_flat, site_matrix, precision=highest)
    second_section = second_flat.reshape(block_rows, local_cols, bond_width, bond_width)
    back_second = jnp.einsum(
        "adk,cgk->acdg",
        left_isometry,
        lax.all_gather(cotangent, "row", axis=2, tiled=True),
        precision=highest,
    )
    left_terms = jnp.einsum(
        "acdg,cgk->adk",
        second_section,
        lax.all_gather(cotangent, "row", axis=2, tiled=True),
        precision=highest,
    )
    back_flat = back_second.reshape(block_rows, local_cols, square)
    back_first = jnp.dot(back_flat, site_matrix.T, precision=highest).reshape(
        block_rows, local_cols, bond_width, bond_width
    )
    site_terms = jnp.dot(
        first_flat.reshape(-1, square).T, back_flat.reshape(-1, square), precision=highest
    )
    edge_terms = jnp.einsum("acef,cfb->aeb", back_first, right_whole, precision=highest)
    right_terms = jnp.einsum("aeb,acef->cfb", edge_tensor, back_first, precision=highest)
    left_gradient, edge_gradient = (
        lax.psum_scatter(left_terms, "col", scatter_dimension=1, tiled=True),
        lax.psum_scatter(edge_terms, "col", scatter_dimension=1, tiled=True),
    )
    right_gradient = lax.psum_scatter(right_terms, "row", scatter_dimension=1, tiled=True)
    site_total = lax.psum(site_terms, ("row", "col"))
    site_gradient = jnp.transpose(
        site_total.reshape(bond_width, bond_width, bond_width, bond_width), (2, 0, 1, 3)
    )
    return (edge_gradient, site_gradient, left_gradient, right_gradient)


def solution(mesh):
    in_specs = (
        P("row", None, None),
        P(),
        P("row", None, None),
        P("col", None, "row"),
        P("col", None, "row"),
    )
    out_specs = (P("row", "col", None), P(), P("row", "col", None), P("col", "row", None))
    return jax.shard_map(
        on_device, mesh=mesh, in_specs=in_specs, out_specs=out_specs, check_vma=False
    )
```

profile of v0, /device:TPU:0, one launch (start us, length us, event | category | flops | bytes accessed | tf_op | source)
XLA Modules:
  0.0 833.3 jit_solution(14730969619415218272)
XLA Ops:
  7.2 0.0 all-gather.3.cloned.1.call-start
  7.2 2.5 copy.22
  9.8 0.0 all-gather.5.cloned.1.call-start
  9.8 2.5 copy.26
  12.4 0.0 reduce-scatter.8.cloned.1.call-start
  12.4 56.7 %all-gather.3.cloned.1.call-done = f32[128,16,1024]{2,0,1:T(8,128)} async-done(((f32[128,16,128]{2,0,1:T(8,128)}), f32[128,16,1024]{2,0,1:T(8,128)}) %all-gather.3.cloned.1.call-update) | async-done | bytes 8388624 | tf_op jit(solution)/shard_map/all_gather | solution.py:22
  69.1 74.2 %fusion.12 = f32[128,16,128,16]{2,0,3,1:T(8,128)} fusion(f32[128,16,1024]{2,0,1:T(8,128)} %all-gather.3.cloned.1.call-done, f32[128,16,1024]{2,1,0:T(8,128)} %param.7), kind=kOutput, calls=%fused_computation.14 | convolution fusion | flops 51539607552 | bytes 33554432 | tf_op jit(solution)/shard_map/adk,cgk->acdg/dot_general | solution.py:19
  143.4 17.8 %copy.41 = f32[128,128,16,16,1]{1,3,2,4,0:T(8,128)} copy(f32[128,128,16,16,1]{0,1,2,3,4:T(8,128)} %bitcast.92) | data formatting | bytes 33554432 | tf_op jit(solution)/shard_map/adk,cgk->acdg/transpose | solution.py:19
  161.2 31.1 %convolution_bitcast_fusion.1 = f32[128,128,16,16]{1,3,2,0:T(8,128)} fusion(f32[128,128,16,16,1]{1,3,2,4,0:T(8,128)} %copy.41, f32[16,16,16,16]{3,2,1,0:T(8,128)S(1)} %copy-done), kind=kOutput, calls=%fused_computation.12 | convolution fusion | flops 12884901888 | bytes 33816576 | tf_op jit(solution)/shard_map/dot_general | solution.py:32
  192.3 66.7 %fusion.31 = f32[128,16,1024]{2,0,1:T(8,128)} fusion(f32[128,16,1024]{2,1,0:T(8,128)} %param.5, f32[128,128,16,16]{1,3,2,0:T(8,128)} %convolution_bitcast_fusion.1), kind=kOutput, calls=%fused_computation.25 | convolution fusion | flops 51539607552 | bytes 33554432 | tf_op jit(solution)/shard_map/aeb,acef->cfb/dot_general | solution.py:39
  259.0 0.0 reduce-scatter.4.cloned.1.call-start
  259.1 79.3 %fusion.21 = f32[128,16,1024]{2,0,1:T(8,128)} fusion(f32[128,16,1024]{2,0,1:T(8,128)} %all-gather.5.cloned.1.call-done, f32[128,128,16,16]{1,3,2,0:T(8,128)} %convolution_bitcast_fusion.1), kind=kOutput, calls=%fused_computation.23 | convolution fusion | flops 51539607552 | bytes 33554432 | tf_op jit(solution)/shard_map/acef,cfb->aeb/dot_general | solution.py:38
  338.4 0.0 reduce-scatter.6.cloned.1.call-start
  338.5 2.8 copy.33
  341.3 0.9 reshape.25
  342.2 0.1 copy.34
  342.4 75.3 %convolution_bitcast_fusion = f32[128,128,16,16]{0,1,2,3:T(8,128)} fusion(f32[128,16,1024]{2,0,1:T(8,128)} %all-gather.5.cloned.1.call-done, f32[128,16,1024]{2,1,0:T(8,128)} %param.5), kind=kOutput, calls=%fused_computation.11 | convolution fusion | flops 51539607552 | bytes 33554432 | tf_op jit(solution)/shard_map/aeb,cfb->acef/dot_general | solution.py:15
  417.7 17.7 %copy.32 = f32[128,128,16,16]{1,3,2,0:T(8,128)} copy(f32[128,128,16,16]{0,1,2,3:T(8,128)} %convolution_bitcast_fusion) | data formatting | bytes 33554432 | tf_op jit(solution)/shard_map/aeb,cfb->acef/transpose | solution.py:15
  435.4 22.3 %fusion.38 = f32[128,128,16,16]{1,3,2,0:T(8,128)} fusion(f32[128,128,256,1]{1,2,3,0:T(8,128)} %bitcast.94, f32[16,16,256,1]{2,1,0,3:T(8,128)S(1)} %bitcast.97), kind=kOutput, calls=%fused_computation.29 | convolution fusion | flops 12884901888 | bytes 33816576 | tf_op jit(solution)/shard_map/dot_general | solution.py:17
  457.7 79.4 %fusion.26 = f32[128,16,1024]{2,0,1:T(8,128)} fusion(f32[128,16,1024]{2,0,1:T(8,128)} %all-gather.3.cloned.1.call-done, f32[128,128,16,16]{1,3,2,0:T(8,128)} %fusion.38), kind=kOutput, calls=%fused_computation.24 | convolution fusion | flops 51539607552 | bytes 33554432 | tf_op jit(solution)/shard_map/acdg,cgk->adk/dot_general | solution.py:25
  537.1 0.0 all-reduce.2.cloned.1.call-start
  537.2 18.0 %copy.29 = f32[128,128,16,16]{1,0,3,2:T(8,128)} copy(f32[128,128,16,16]{0,1,2,3:T(8,128)} %convolution_bitcast_fusion) | data formatting | bytes 33554432 | tf_op jit(solution)/shard_map/aeb,cfb->acef/transpose | solution.py:15
  555.2 17.7 %copy.30 = f32[128,128,16,16]{1,0,3,2:T(8,128)} copy(f32[128,128,16,16]{0,1,2,3:T(8,128)} %bitcast.93) | data formatting | bytes 33554432 | tf_op jit(solution)/shard_map/adk,cgk->acdg/transpose | solution.py:19
  572.8 40.3 %fusion = f32[256,256]{1,0:T(8,128)S(1)} fusion(f32[32,8,128,128]{3,2,1,0:T(8,128)} %bitcast.91, f32[32,8,128,128]{3,2,1,0:T(8,128)} %bitcast.90), kind=kOutput, calls=%fused_computation | convolution fusion | flops 12884901888 | bytes 33816576 | tf_op jit(solution)/shard_map/dot_general | solution.py:35
  613.2 0.6 reshape.23
  613.8 2.0 copy.92
  615.8 3.0 copy.39
  618.8 4.3 copy.37
  623.1 58.6 %reduce-scatter.6.cloned.1.call-done = f32[128,4,1024]{2,0,1:T(8,128)} async-done(((f32[128,16,1024]{2,0,1:T(8,128)}), f32[128,4,1024]{2,0,1:T(8,128)}) %reduce-scatter.6.cloned.1.call-update) | async-done | bytes 2097168 | tf_op jit(solution)/shard_map/reduce_scatter | solution.py:41
  681.7 4.3 copy.38
  686.0 136.9 %all-reduce.2.cloned.1.call-done = f32[16,16,16,16]{3,2,1,0:T(8,128)} async-done(((f32[16,16,16,16]{3,2,1,0:T(8,128)}), f32[16,16,16,16]{3,2,1,0:T(8,128)}) %all-reduce.2.cloned.1.call-update) | async-done | bytes 262160 | tf_op jit(solution)/shard_map/psum | solution.py:45
  822.9 3.1 copy.94
  (11 shorter events, 0.1 us)
Async XLA Ops:
  7.2 62.0 %all-gather.3.cloned.1.call-start = ((), (), s32[]{:S(2)}) async-start(), calls=%async_computation.3 | async-start | bytes 9437184 | tf_op jit(solution)/shard_map/all_gather | solution.py:22
  9.8 249.3 %all-gather.5.cloned.1.call-start = ((), (), s32[]{:S(2)}) async-start(), calls=%async_computation.4 | async-start | bytes 9437184 | tf_op jit(solution)/shard_map/all_gather | solution.py:14
  12.4 603.4 %reduce-scatter.8.cloned.1.call-start = ((), (), s32[]{:S(2)}) async-start(), calls=%async_computation.8 | async-start | bytes 9437184 | tf_op jit(solution)/shard_map/reduce_scatter | solution.py:44
  143.4 17.8 %copy-start = (f32[16,16,16,16]{3,2,1,0:T(8,128)S(1)}, f32[16,16,16,16]{3,2,1,0:T(8,128)}, u32[]{:S(2)}) copy-start(f32[16,16,16,16]{3,2,1,0:T(8,128)} %param.6) | copy-start | bytes 786436
  259.0 359.8 %reduce-scatter.4.cloned.1.call-start = ((), (), s32[]{:S(2)}) async-start(), calls=%async_computation.5 | async-start | bytes 10485760 | tf_op jit(solution)/shard_map/reduce_scatter | solution.py:42
  338.4 343.3 %reduce-scatter.6.cloned.1.call-start = ((), (), s32[]{:S(2)}) async-start(), calls=%async_computation.7 | async-start | bytes 10485760 | tf_op jit(solution)/shard_map/reduce_scatter | solution.py:41
  537.1 285.8 %all-reduce.2.cloned.1.call-start = ((), (), s32[]{:S(2)}) async-start(), calls=%async_computation.6 | async-start | bytes 4194304 | tf_op jit(solution)/shard_map/psum | solution.py:45
Sparse Core Ops, SparseCore 0:
  10.4 58.6 all-gather.2
  71.6 55.9 all-gather.4
  259.1 71.2 reduce-scatter.7
  338.6 144.4 reduce-scatter.3
  537.2 144.4 reduce-scatter.5
  688.4 134.4 all-reduce.1
where the time goes:
time: 846 us; the launch traced here: 833 us
  matrix products  469 us (55%)
  waiting for transfers between devices  252 us (30%)
  local copies, waits for them, and re-layouts  97.4 us (12%)
  between operations  14.6 us (2%)
    psum x1, waiting for transfers between devices, on_device(): site_total = lax.psum(site_terms, ('row', 'col'))  137 us
    dot_general x1, matrix products, on_device(): jnp.einsum('acdg,cgk->adk', second_section, lax.all_gather(cotangent, 'ro...  79.4 us
    dot_general x1, matrix products, on_device(): jnp.einsum('acef,cfb->aeb', back_first, right_whole, precision=highest)  79.3 us
    dot_general x1, matrix products, on_device(): jnp.einsum('aeb,cfb->acef', edge_tensor, right_whole, precision=highest)  75.3 us
    dot_general x1, matrix products, on_device(): jnp.einsum('adk,cgk->acdg', left_isometry, lax.all_gather(cotangent, 'row...  74.2 us
    dot_general x1, matrix products, on_device(): jnp.einsum('aeb,acef->cfb', edge_tensor, back_first, precision=highest)  66.7 us
    reduce_scatter x1, waiting for transfers between devices, on_device(): lax.psum_scatter(left_terms, 'col', scatter_dimension=1, tiled=True)  58.6 us
    all_gather x1, waiting for transfers between devices, on_device(): lax.all_gather(cotangent, 'row', axis=2, tiled=True)  56.7 us
  transfers between devices with their start and end apart: 6, of which 3 were waited for; matrix products, arithmetic and copies ran while one was open for 67% of the time, Pallas kernels for 0%

commit v1 on v0

v1 whole, which is shorter than its diff:
```python
import functools

import jax
import jax.numpy as jnp
from jax import lax
from jax.experimental import pallas as pl
from jax.experimental.pallas import tpu as pltpu
from jax.sharding import PartitionSpec as P

F32 = jnp.float32
BF16 = jnp.bfloat16
HIGH = lax.Precision.HIGH
NN = (((1,), (0,)), ((), ()))
NT = (((1,), (1,)), ((), ()))
TN = (((0,), (0,)), ((), ()))
BLOCK = 256
TILE = 512


def halves(x):
    hi = x.astype(BF16)
    return hi, (x - hi.astype(F32)).astype(BF16)


def split(x):
    hi = lax.reduce_precision(x, 8, 7)
    return hi.astype(BF16), (x - hi).astype(BF16)


def dot3(xh, xl, yh, yl, dims):
    def dot(x, y):
        return lax.dot_general(x, y, dims, preferred_element_type=F32)

    return dot(xh, yh) + dot(xh, yl) + dot(xl, yh)


def project(xh, xl, wh_ref, wl_ref, oh_ref, ol_ref):
    n = wh_ref.shape[0]
    tile = min(TILE, n)

    def step(i, carry):
        cols = pl.ds(pl.multiple_of(i * tile, tile), tile)
        hi, lo = halves(dot3(xh, xl, wh_ref[cols, :], wl_ref[cols, :], NT))
        oh_ref[:, cols] = hi
        ol_ref[:, cols] = lo
        return carry

    lax.fori_loop(0, n // tile, step, 0)


def gather_pair(ref, start, d, s):
    parts = []
    for k in range(2):
        rows = ref[pl.ds(pl.multiple_of(start + k * d, d), d), :]
        parts.append(jnp.concatenate([rows[:, j * s : (j + 1) * s] for j in range(d)], axis=0))
    return jnp.concatenate(parts, axis=1)


def spread_pair(ref, value, start, d, s):
    for k in range(2):
        rows = [value[j * d : (j + 1) * d, k * s : (k + 1) * s] for j in range(d)]
        ref[pl.ds(pl.multiple_of(start + k * d, d), d), :] = jnp.concatenate(rows, axis=1)


def combine(xh_ref, xl_ref, wh_ref, wl_ref, o_ref):
    n = wh_ref.shape[1]
    tile = min(TILE // 2, n)

    def step(i, carry):
        cols = pl.ds(pl.multiple_of(i * tile, tile), tile)
        o_ref[:, cols] = dot3(xh_ref[...], xl_ref[...], wh_ref[:, cols], wl_ref[:, cols], NN)
        return carry

    lax.fori_loop(0, n // tile, step, 0)


def forward_kernel(d, s, e_ref, sh_ref, sl_ref, rh_ref, rl_ref, ch_ref, cl_ref, left_ref, fh_ref, fl_ref, gh, gl):
    eh, el = halves(e_ref[...])
    project(eh, el, rh_ref, rl_ref, fh_ref, fl_ref)

    def step(i, carry):
        start = i * 2 * d
        x = gather_pair(fh_ref, start, d, s), gather_pair(fl_ref, start, d, s)
        hi, lo = halves(dot3(sh_ref[...], sl_ref[...], *x, NN))
        spread_pair(gh, hi, start, d, s)
        spread_pair(gl, lo, start, d, s)
        return carry

    lax.fori_loop(0, e_ref.shape[0] // (2 * d), step, 0)
    combine(gh, gl, ch_ref, cl_ref, left_ref)


def backward_kernel(
    d, s, e_ref, l_ref, fh_ref, fl_ref, sh_ref, sl_ref, rh_ref, rl_ref, ch_ref, cl_ref,
    edge_ref, right_ref, site_ref, bh, bl, gh, gl,
):
    @pl.when(pl.program_id(0) == 0)
    def _():
        right_ref[...] = jnp.zeros_like(right_ref)
        site_ref[...] = jnp.zeros_like(site_ref)

    lh, ll = halves(l_ref[...])
    project(lh, ll, ch_ref, cl_ref, bh, bl)

    def step(i, carry):
        start = i * 2 * d
        x = gather_pair(bh, start, d, s), gather_pair(bl, start, d, s)
        y = gather_pair(fh_ref, start, d, s), gather_pair(fl_ref, start, d, s)
        hi, lo = halves(dot3(sh_ref[...], sl_ref[...], *x, NN))
        spread_pair(gh, hi, start, d, s)
        spread_pair(gl, lo, start, d, s)
        site_ref[...] += dot3(*x, *y, NT)
        return carry

    lax.fori_loop(0, e_ref.shape[0] // (2 * d), step, 0)
    combine(gh, gl, rh_ref, rl_ref, edge_ref)
    eh, el = halves(e_ref[...])
    tile = min(BLOCK, gh.shape[1])

    def add(i, carry):
        cols = pl.ds(pl.multiple_of(i * tile, tile), tile)
        right_ref[cols, :] += dot3(gh[:, cols], gl[:, cols], eh, el, TN)
        return carry

    lax.fori_loop(0, gh.shape[1] // tile, add, 0)


def whole(shape):
    return pl.BlockSpec(shape, lambda i: (0, 0), pipeline_mode=pl.Buffered(1))


def rows_of(width):
    return pl.BlockSpec((BLOCK, width), lambda i: (i, 0))


PARAMS = pltpu.CompilerParams(dimension_semantics=("arbitrary",), vmem_limit_bytes=58 * 2**20)


def forward(edge, site, right, cot, d, s):
    rows, chi = edge.shape
    wide = d * s
    return pl.pallas_call(
        functools.partial(forward_kernel, d, s),
        grid=(rows // BLOCK,),
        out_shape=[
            jax.ShapeDtypeStruct((rows, chi), F32),
            jax.ShapeDtypeStruct((rows, wide), BF16),
            jax.ShapeDtypeStruct((rows, wide), BF16),
        ],
        in_specs=[rows_of(chi)] + [whole((d * d, d * d))] * 2 + [whole((wide, chi))] * 4,
        out_specs=[rows_of(chi), rows_of(wide), rows_of(wide)],
        scratch_shapes=[pltpu.VMEM((BLOCK, wide), BF16)] * 2,
        compiler_params=PARAMS,
        cost_estimate=pl.CostEstimate(
            flops=12 * rows * wide * chi, bytes_accessed=8 * (rows + wide) * chi, transcendentals=0
        ),
        name="forward",
    )(edge, *site, *right, *cot)


def backward(edge, left, first, site, right, cot, d, s):
    rows, chi = edge.shape
    wide = d * s
    return pl.pallas_call(
        functools.partial(backward_kernel, d, s),
        grid=(rows // BLOCK,),
        out_shape=[
            jax.ShapeDtypeStruct((rows, chi), F32),
            jax.ShapeDtypeStruct((wide, chi), F32),
            jax.ShapeDtypeStruct((d * d, d * d), F32),
        ],
        in_specs=[rows_of(chi)] * 2 + [rows_of(wide)] * 2 + [whole((d * d, d * d))] * 2 + [whole((wide, chi))] * 4,
        out_specs=[rows_of(chi), whole((wide, chi)), whole((d * d, d * d))],
        scratch_shapes=[pltpu.VMEM((BLOCK, wide), BF16)] * 4,
        compiler_params=PARAMS,
        cost_estimate=pl.CostEstimate(
            flops=20 * rows * wide * chi, bytes_accessed=8 * (rows + wide) * chi, transcendentals=0
        ),
        name="backward",
    )(edge, left, *first, *site, *right, *cot)


def swap(x, axis, bit):
    n = lax.axis_size(axis)
    return lax.ppermute(x, axis, [(i, i ^ bit) for i in range(n)])


def gather_row(x):
    s, f, k = x.shape
    n = lax.axis_size("row")
    x = jnp.transpose(x, (1, 0, 2)).reshape(f * s, k)
    groups = [list(range(c, n, 2)) for c in range(2)]
    mine = lax.all_gather(x, "row", axis=0, axis_index_groups=groups)
    other = swap(mine, "row", 1)
    first_core = lax.rem(lax.axis_index("row"), 2) == 0
    even = jnp.where(first_core, mine, other)
    odd = jnp.where(first_core, other, mine)
    return jnp.transpose(jnp.stack([even, odd], 1), (2, 0, 1, 3)).reshape(f * s, n * k)


def sum_to_row(x):
    n = lax.axis_size("row")
    me = lax.axis_index("row")
    x = x.reshape((n, -1) + x.shape[1:])
    bit = 1
    while bit < n:
        x = x.reshape((x.shape[0] // 2, 2) + x.shape[1:])
        mine = lax.rem(me // bit, 2)
        keep = lax.dynamic_index_in_dim(x, mine, 1, keepdims=False)
        send = lax.dynamic_index_in_dim(x, 1 - mine, 1, keepdims=False)
        x = keep + swap(send, "row", bit)
        bit *= 2
    return x[0]


def sum_all(x):
    for axis in ("row", "col"):
        bit = 1
        while bit < lax.axis_size(axis):
            x = x + swap(x, axis, bit)
            bit *= 2
    return x


def with_kernels(edge_tensor, site_tensor, left_isometry, right_isometry, cotangent, n_front=4, n_back=2):
    a, d, chi = edge_tensor.shape
    s = right_isometry.shape[0]
    right = split(gather_row(right_isometry))
    cot = split(gather_row(cotangent))
    site_front = split(jnp.transpose(site_tensor, (3, 0, 2, 1)).reshape(d * d, d * d))
    site_back = split(jnp.transpose(site_tensor, (2, 1, 3, 0)).reshape(d * d, d * d))
    edge = edge_tensor.reshape(a * d, chi)
    left = left_isometry.reshape(a * d, chi)

    def scatter(terms):
        return lax.psum_scatter(terms.reshape(-1, d, chi), "col", scatter_dimension=1, tiled=True)

    n_front = min(n_front, a * d // BLOCK)
    n_back = min(n_back, n_front)
    lefts, firsts = [], []
    for x in jnp.split(edge, n_front):
        terms, fh, fl = forward(x, site_front, right, cot, d, s)
        lefts.append(scatter(terms))
        firsts.append((fh, fl))
    join = n_front // n_back
    edges, rights, sites = [], [], []
    for i, (x, y) in enumerate(zip(jnp.split(edge, n_back), jnp.split(left, n_back))):
        part = firsts[i * join : (i + 1) * join]
        first = tuple(jnp.concatenate([p[k] for p in part], 0) for k in range(2))
        edge_terms, right_terms, site_terms = backward(x, y, first, site_back, right, cot, d, s)
        edges.append(scatter(edge_terms))
        rights.append(right_terms)
        sites.append(site_terms)
    right_sum = sum_to_row(sum(rights))
    right_gradient = jnp.transpose(right_sum.reshape(-1, s, chi), (1, 0, 2))
    site_gradient = jnp.transpose(sum_all(sum(sites)).reshape(d, d, d, d), (1, 3, 2, 0))
    return jnp.concatenate(edges, 0), site_gradient, jnp.concatenate(lefts, 0), right_gradient


def ein(spec, x, y):
    return jnp.einsum(spec, x, y, precision=HIGH)


def without_kernels(edge_tensor, site_tensor, left_isometry, right_isometry, cotangent):
    edge = jnp.transpose(edge_tensor, (1, 0, 2))
    left = jnp.transpose(left_isometry, (1, 0, 2))
    right = lax.all_gather(jnp.transpose(right_isometry, (1, 0, 2)), "row", axis=2, tiled=True)
    cot = lax.all_gather(jnp.transpose(cotangent, (1, 0, 2)), "row", axis=2, tiled=True)
    first = ein("eab,fsb->efas", edge, right)
    second = ein("defg,efas->dgas", site_tensor, first)
    left_terms = ein("dgas,gsc->dac", second, cot)
    left_gradient = lax.psum_scatter(left_terms, "col", scatter_dimension=0, tiled=True)
    back_second = ein("dac,gsc->dgas", left, cot)
    back_first = ein("defg,dgas->efas", site_tensor, back_second)
    edge_terms = ein("efas,fsb->eab", back_first, right)
    edge_gradient = lax.psum_scatter(edge_terms, "col", scatter_dimension=0, tiled=True)
    right_terms = ein("efas,eab->sfb", back_first, edge)
    right_gradient = lax.psum_scatter(right_terms, "row", scatter_dimension=1, tiled=True)
    site_terms = ein("efas,dgas->efdg", first, back_second)
    site_gradient = jnp.transpose(lax.psum(site_terms, ("row", "col")), (2, 0, 1, 3))
    return (
        jnp.transpose(edge_gradient, (1, 0, 2)),
        site_gradient,
        jnp.transpose(left_gradient, (1, 0, 2)),
        right_gradient,
    )


def on_device(*args):
    a, d, chi = args[0].shape
    s = args[3].shape[0]
    n_row, n_col = lax.axis_size("row"), lax.axis_size("col")
    fits = s % 128 == 0 and chi % 256 == 0 and (a * d) % BLOCK == 0 and d % 16 == 0 and n_row > 1
    fits = fits and n_row & (n_row - 1) == 0 and n_col & (n_col - 1) == 0
    fits = fits and 16 * d * s * chi + 4 * d * s * chi <= 42 * 2**20
    return with_kernels(*args) if fits else without_kernels(*args)


def solution(mesh):
    in_specs = (
        P("row", None, None),
        P(),
        P("row", None, None),
        P("col", None, "row"),
        P("col", None, "row"),
    )
    out_specs = (P("row", "col", None), P(), P("row", "col", None), P("col", "row", None))
    return jax.shard_map(
        on_device, mesh=mesh, in_specs=in_specs, out_specs=out_specs, check_vma=False
    )
```

time: 846 us -> 731 us (0.86)
  matrix products: 469 us -> 0 us
  Pallas kernels: 0 us -> 274 us
  other arithmetic: 0 us -> 66 us
  local copies, waits for them, and re-layouts: 97.4 us -> 157 us
  waiting for transfers between devices: 252 us -> 200 us
  starting transfers between devices: 0.25 us -> 9.46 us
    dot_general x8 -> x0, matrix products: 469 us -> none  [the longest x1 79.4 us: on_device(): jnp.einsum('acdg,cgk->adk', second_section, lax.all_gather(cotangent, 'ro...]
    pallas_call x0 -> x6, Pallas kernels: none -> 274 us  [the longest x2 157 us: backward(): pl.pallas_call(functools.partial(backward_kernel, d, s), grid=(rows // BL...]
    psum x1 -> x0, waiting for transfers between devices: 137 us -> none  [on_device(): site_total = lax.psum(site_terms, ('row', 'col'))]
    ppermute x0 -> x10, waiting for transfers between devices: none -> 91.3 us  [swap(): return lax.ppermute(x, axis, [(i, i ^ bit) for i in range(n)])]
    reduce_scatter x3 -> x6, waiting for transfers between devices: 58.6 us -> 0.02 us  [scatter(): lax.psum_scatter(terms.reshape(-1, d, chi), 'col', scatter_dimension=1, t...]
    reshape x3 -> x12, local copies, waits for them, and re-layouts: 3.54 us -> 62 us  [the longest x6 27.9 us: scatter(): terms.reshape(-1, d, chi)]
    all_gather x2, waiting for transfers between devices: 56.7 us -> 108 us  [gather_row(): mine = lax.all_gather(x, 'row', axis=0, axis_index_groups=groups)]
    transpose x5 -> x4, local copies, waits for them, and re-layouts: 74 us -> 48 us  [the longest x2 33 us: gather_row(): jnp.transpose(jnp.stack([even, odd], 1), (2, 0, 1, 3)).reshape(f * s, n * k)]
  transfers between devices with their start and end apart: 6 -> 18, of which waited for: 3 -> 9; matrix products, arithmetic and copies ran while one was open for 67% -> 18% of each run, Pallas kernels for 0% -> 34%
where the time goes in v1:
time: 731 us; the launch traced here: 721 us
  Pallas kernels  274 us (37%)
  waiting for transfers between devices  200 us (27%)
  local copies, waits for them, and re-layouts  157 us (21%)
  other arithmetic  66 us (9%)
  between operations  14.8 us (2%)
  starting transfers between devices  9.46 us (1%)
    pallas_call x2, Pallas kernels, backward(): pl.pallas_call(functools.partial(backward_kernel, d, s), grid=(rows // BL...  157 us
    pallas_call x4, Pallas kernels, forward(): pl.pallas_call(functools.partial(forward_kernel, d, s), grid=(rows // BLO...  117 us
    all_gather x2, waiting for transfers between devices, gather_row(): mine = lax.all_gather(x, 'row', axis=0, axis_index_groups=groups)  108 us
    ppermute x10, waiting for transfers between devices, swap(): return lax.ppermute(x, axis, [(i, i ^ bit) for i in range(n)])  91.3 us
    transpose x2, local copies, waits for them, and re-layouts, gather_row(): jnp.transpose(jnp.stack([even, odd], 1), (2, 0, 1, 3)).reshape(f * s, n * k)  33 us
    reshape x6, local copies, waits for them, and re-layouts, scatter(): terms.reshape(-1, d, chi)  27.9 us
    reshape x2, local copies, waits for them, and re-layouts, gather_row(): jnp.transpose(jnp.stack([even, odd], 1), (2, 0, 1, 3)).reshape(f * s, n * k)  23.4 us
    convert_element_type x4, other arithmetic, split(): return (hi.astype(BF16), (x - hi).astype(BF16))  18.8 us
  transfers between devices with their start and end apart: 18, of which 9 were waited for; matrix products, arithmetic and copies ran while one was open for 18% of the time, Pallas kernels for 34%

profile of v1, /device:TPU:0, one launch (start us, length us, event | category | flops | bytes accessed | tf_op | source)
XLA Modules:
  0.0 721.4 jit_solution(16313128010848805215)
XLA Ops:
  12.6 53.3 %all-gather.5.cloned.1.call-done = f32[4,2048,128]{2,1,0:T(8,128)} async-done(((f32[1,2048,128]{2,1,0:T(8,128)}), f32[4,2048,128]{2,1,0:T(8,128)}) %all-gather.5.cloned.1.call-update) | async-done | bytes 4194320 | tf_op jit(solution)/shard_map/all_gather | solution.py:193
  65.9 55.2 %all-gather.3.cloned.1.call-done = f32[4,2048,128]{2,1,0:T(8,128)} async-done(((f32[1,2048,128]{2,1,0:T(8,128)}), f32[4,2048,128]{2,1,0:T(8,128)}) %all-gather.3.cloned.1.call-update) | async-done | bytes 4194320 | tf_op jit(solution)/shard_map/all_gather | solution.py:193
  127.0 7.8 %fusion.4 = (f32[32,16,1024]{2,1,0:T(8,128)}, f32[32,16,1024]{2,1,0:T(8,128)}, f32[32,16,1024]{2,1,0:T(8,128)}, f32[32,16,1024]{2,1,0:T(8,128)}) fusion(f32[128,16,1024]{2,1,0:T(8,128)} %param.5), kind=kLoop, calls=%fused_computation.30 | loop fusion | bytes 16777216 | tf_op jit(solution)/shard_map/split | solution.py:241
  135.3 6.0 select_bitcast_fusion.1
  141.9 16.5 %copy.32 = f32[2048,4,2,128]{3,2,1,0:T(2,128)} copy(f32[2048,4,2,128]{3,0,1,2:T(8,128)S(1)} %maximum_bitcast_fusion) | data formatting | bytes 16777216 | tf_op jit(solution)/shard_map/transpose | solution.py:198
  158.4 11.6 %reshape.60 = f32[2048,1024]{1,0:T(8,128)} reshape(f32[2048,4,2,128]{3,2,1,0:T(2,128)} %copy.32) | data formatting | bytes 16777216 | tf_op jit(solution)/shard_map/reshape | solution.py:198
  170.0 8.8 %fusion = (bf16[2048,1024]{1,0:T(8,128)(2,1)}, bf16[2048,1024]{1,0:T(8,128)(2,1)}) fusion(f32[2048,1024]{1,0:T(8,128)} %reshape.60), kind=kLoop, calls=%fused_computation.4 | loop fusion | flops 8388608 | bytes 16777216 | tf_op jit(solution)/shard_map/convert_element_type | solution.py:27
  179.3 16.5 %copy.34 = f32[2048,4,2,128]{3,2,1,0:T(2,128)} copy(f32[2048,4,2,128]{3,0,1,2:T(8,128)S(1)} %maximum_bitcast_fusion.1) | data formatting | bytes 16777216 | tf_op jit(solution)/shard_map/transpose | solution.py:198
  195.9 11.8 %reshape.61 = f32[2048,1024]{1,0:T(8,128)} reshape(f32[2048,4,2,128]{3,2,1,0:T(2,128)} %copy.34) | data formatting | bytes 16777216 | tf_op jit(solution)/shard_map/reshape | solution.py:198
  207.7 8.6 %fusion.1 = (bf16[2048,1024]{1,0:T(8,128)(2,1)}, bf16[2048,1024]{1,0:T(8,128)(2,1)}) fusion(f32[2048,1024]{1,0:T(8,128)} %reshape.61), kind=kLoop, calls=%fused_computation.5 | loop fusion | flops 8388608 | bytes 16777216 | tf_op jit(solution)/shard_map/convert_element_type | solution.py:27
  216.2 29.2 %forward.7 = (f32[512,1024]{1,0:T(8,128)}, bf16[512,2048]{1,0:T(8,128)(2,1)}, bf16[512,2048]{1,0:T(8,128)(2,1)}) custom-call(f32[512,1024]{1,0:T(8,128)} %bitcast.75, bf16[256,256]{1,0:T(8,128)(2,1)} %get-tuple-element.71.sh_ref, bf16[256,256]{1,0:T(8,128)(2,1)} %get-tuple-element.70.sl_ref, bf16[2048,1024]{1,0:T(8,128)(2,1)} %get-tuple-element.65.rh_ref, ...), custom_call_target="tpu_custom_call" | custom-call | flops 12884901888 | bytes 20971520 | tf_op jit(solution)/shard_map/forward/pallas_call | solution.py:142
  249.7 29.3 %forward.6 = (f32[512,1024]{1,0:T(8,128)}, bf16[512,2048]{1,0:T(8,128)(2,1)}, bf16[512,2048]{1,0:T(8,128)(2,1)}) custom-call(f32[512,1024]{1,0:T(8,128)} %bitcast.74, bf16[256,256]{1,0:T(8,128)(2,1)} %get-tuple-element.71.sh_ref, bf16[256,256]{1,0:T(8,128)(2,1)} %get-tuple-element.70.sl_ref, bf16[2048,1024]{1,0:T(8,128)(2,1)} %get-tuple-element.65.rh_ref, ...), custom_call_target="tpu_custom_call" | custom-call | flops 12884901888 | bytes 20971520 | tf_op jit(solution)/shard_map/forward/pallas_call | solution.py:142
  279.0 4.2 copy.41
  283.3 29.4 %forward.5 = (f32[512,1024]{1,0:T(8,128)}, bf16[512,2048]{1,0:T(8,128)(2,1)}, bf16[512,2048]{1,0:T(8,128)(2,1)}) custom-call(f32[512,1024]{1,0:T(8,128)} %bitcast.73, bf16[256,256]{1,0:T(8,128)(2,1)} %get-tuple-element.71.sh_ref, bf16[256,256]{1,0:T(8,128)(2,1)} %get-tuple-element.70.sl_ref, bf16[2048,1024]{1,0:T(8,128)(2,1)} %get-tuple-element.65.rh_ref, ...), custom_call_target="tpu_custom_call" | custom-call | flops 12884901888 | bytes 20971520 | tf_op jit(solution)/shard_map/forward/pallas_call | solution.py:142
  312.7 4.2 copy.40
  316.9 12.2 %copy.35 = f32[16,16,16,16]{3,2,1,0:T(8,128)} copy(f32[16,16,16,16]{2,0,1,3:T(8,128)S(1)} %bitcast.57) | data formatting | bytes 524288 | tf_op jit(solution)/shard_map/transpose | solution.py:231
  332.3 8.6 %fusion.6 = (f32[64,16,1024]{2,1,0:T(8,128)}, f32[64,16,1024]{2,1,0:T(8,128)}) fusion(f32[128,16,1024]{2,1,0:T(8,128)} %param.5), kind=kLoop, calls=%fused_computation.32 | loop fusion | bytes 16777216 | tf_op jit(solution)/shard_map/split | solution.py:247
  340.8 8.5 %fusion.5 = (f32[64,16,1024]{2,1,0:T(8,128)}, f32[64,16,1024]{2,1,0:T(8,128)}) fusion(f32[128,16,1024]{2,1,0:T(8,128)} %param.7), kind=kLoop, calls=%fused_computation.31 | loop fusion | bytes 16777216 | tf_op jit(solution)/shard_map/split | solution.py:247
  349.4 29.3 %forward.4 = (f32[512,1024]{1,0:T(8,128)}, bf16[512,2048]{1,0:T(8,128)(2,1)}, bf16[512,2048]{1,0:T(8,128)(2,1)}) custom-call(f32[512,1024]{1,0:T(8,128)} %bitcast.72, bf16[256,256]{1,0:T(8,128)(2,1)} %get-tuple-element.71.sh_ref, bf16[256,256]{1,0:T(8,128)(2,1)} %get-tuple-element.70.sl_ref, bf16[2048,1024]{1,0:T(8,128)(2,1)} %get-tuple-element.65.rh_ref, ...), custom_call_target="tpu_custom_call" | custom-call | flops 12884901888 | bytes 20971520 | tf_op jit(solution)/shard_map/forward/pallas_call | solution.py:142
  382.9 4.9 pad_maximum_fusion.2.fh_ref
  392.0 78.4 %backward.3 = (f32[1024,1024]{1,0:T(8,128)}, f32[2048,1024]{1,0:T(8,128)}, f32[256,256]{1,0:T(8,128)}) custom-call(f32[1024,1024]{1,0:T(8,128)} %bitcast.65, f32[1024,1024]{1,0:T(8,128)} %bitcast.66, bf16[1024,2048]{1,0:T(8,128)(2,1)} %pad_maximum_fusion.2.fh_ref, bf16[1024,2048]{1,0:T(8,128)(2,1)} %pad_maximum_fusion.3.fl_ref, ...), custom_call_target="tpu_custom_call" | custom-call | flops 42949672960 | bytes 25165824 | tf_op jit(solution)/shard_map/backward/pallas_call | solution.py:164
  470.4 6.7 copy.37
  478.7 4.3 pad_maximum_fusion.fh_ref
  485.6 78.3 %backward.2 = (f32[1024,1024]{1,0:T(8,128)}, f32[2048,1024]{1,0:T(8,128)}, f32[256,256]{1,0:T(8,128)}) custom-call(f32[1024,1024]{1,0:T(8,128)} %bitcast.63, f32[1024,1024]{1,0:T(8,128)} %bitcast.64, bf16[1024,2048]{1,0:T(8,128)(2,1)} %pad_maximum_fusion.fh_ref, bf16[1024,2048]{1,0:T(8,128)(2,1)} %pad_maximum_fusion.1.fl_ref, ...), custom_call_target="tpu_custom_call" | custom-call | flops 42949672960 | bytes 25165824 | tf_op jit(solution)/shard_map/backward/pallas_call | solution.py:164
  563.9 12.0 %add.75 = f32[2048,1024]{1,0:T(8,128)} add(f32[2048,1024]{1,0:T(8,128)} %get-tuple-element.38, f32[2048,1024]{1,0:T(8,128)} %get-tuple-element.39) | non-fusion elementwise | flops 2097152 | bytes 25165824 | tf_op jit(solution)/shard_map/add | solution.py:254
  576.0 4.9 dynamic-slice_bitcast_fusion
  581.5 4.5 copy.36
  588.6 4.5 bitcast_add_fusion
  599.0 44.8 %collective-permute-done.8 = f32[2,256,1024]{2,1,0:T(8,128)} collective-permute-done((f32[2,256,1024]{2,1,0:T(8,128)S(1)}, f32[2,256,1024]{2,1,0:T(8,128)}, u32[]{:S(2)}, u32[]{:S(2)}) %collective-permute-start.8) | collective-permute-done | bytes 2097184 | tf_op jit(solution)/shard_map/ppermute | solution.py:185
  650.2 27.3 %collective-permute-done.4 = f32[256,256]{1,0:T(8,128)S(1)} collective-permute-done((f32[256,256]{1,0:T(8,128)S(1)}, f32[256,256]{1,0:T(8,128)S(1)}, u32[]{:S(2)}, u32[]{:S(2)}) %collective-permute-start.4) | collective-permute-done | bytes 262176 | tf_op jit(solution)/shard_map/ppermute | solution.py:185
  678.7 5.3 collective-permute-done.5
  686.5 9.7 %collective-permute-done.6 = f32[256,256]{1,0:T(8,128)S(1)} collective-permute-done((f32[256,256]{1,0:T(8,128)S(1)}, f32[256,256]{1,0:T(8,128)S(1)}, u32[]{:S(2)}, u32[]{:S(2)}) %collective-permute-start.6) | collective-permute-done | bytes 262176 | tf_op jit(solution)/shard_map/ppermute | solution.py:185
  (94 shorter events, 70.0 us)
Async XLA Ops:
  7.2 113.9 %copy-start.3 = (f32[16,16,16,16]{3,2,1,0:T(8,128)S(1)}, f32[16,16,16,16]{3,2,1,0:T(8,128)}, u32[]{:S(2)}) copy-start(f32[16,16,16,16]{3,2,1,0:T(8,128)} %param.6) | copy-start | bytes 786436
  7.2 58.7 %all-gather.5.cloned.1.call-start = ((), (), s32[]{:S(2)}) async-start(), calls=%async_computation.7 | async-start | bytes 5242880 | tf_op jit(solution)/shard_map/all_gather | solution.py:193
  9.9 111.1 %all-gather.3.cloned.1.call-start = ((), (), s32[]{:S(2)}) async-start(), calls=%async_computation.6 | async-start | bytes 5242880 | tf_op jit(solution)/shard_map/all_gather | solution.py:193
  12.5 689.6 %reduce-scatter.17.cloned.1.call-start = ((), (), s32[]{:S(2)}) async-start(), calls=%async_computation.13 | async-start | bytes 2621440 | tf_op jit(solution)/shard_map/reduce_scatter | solution.py:236
  65.9 68.9 %collective-permute-start.1 = (f32[4,2048,128]{2,1,0:T(8,128)}, f32[4,2048,128]{2,1,0:T(8,128)}, u32[]{:S(2)}, u32[]{:S(2)}) collective-permute-start(f32[4,2048,128]{2,1,0:T(8,128)} %all-gather.5.cloned.1.call-done), channel_id=1, source_target_pairs={{0,4},{4,0},{8,12},{12,8},{16,20},{20,16},{24,28},{28,24},{1,5},{5... | collective-permute-start | bytes 12582920 | tf_op jit(solution)/shard_map/ppermute | solution.py:185
  121.0 13.8 %collective-permute-start = (f32[4,2048,128]{2,1,0:T(8,128)}, f32[4,2048,128]{2,1,0:T(8,128)}, u32[]{:S(2)}, u32[]{:S(2)}) collective-permute-start(f32[4,2048,128]{2,1,0:T(8,128)} %all-gather.3.cloned.1.call-done), channel_id=1, source_target_pairs={{0,4},{4,0},{8,12},{12,8},{16,20},{20,16},{24,28},{28,24},{1,5},{5... | collective-permute-start | bytes 12582920 | tf_op jit(solution)/shard_map/ppermute | solution.py:185
  127.0 7.8 %copy-start.4 = (f32[4,2048,128]{2,1,0:T(8,128)S(1)}, f32[4,2048,128]{2,1,0:T(8,128)}, u32[]{:S(2)}) copy-start(f32[4,2048,128]{2,1,0:T(8,128)} %all-gather.5.cloned.1.call-done) | copy-start | bytes 12582916
  127.0 8.3 %copy-start.5 = (f32[4,2048,128]{2,1,0:T(8,128)S(1)}, f32[4,2048,128]{2,1,0:T(8,128)}, u32[]{:S(2)}) copy-start(f32[4,2048,128]{2,1,0:T(8,128)} %all-gather.3.cloned.1.call-done) | copy-start | bytes 12582916
  170.0 8.8 %copy-start.1 = (f32[4,1,2048,128]{3,2,0,1:T(8,128)S(1)}, f32[4,1,2048,128]{3,2,0,1:T(8,128)}, u32[]{:S(2)}) copy-start(f32[4,1,2048,128]{3,2,0,1:T(8,128)} %get-tuple-element.62) | copy-start | bytes 12582916
  170.0 8.8 %copy-start.2 = (f32[4,1,2048,128]{3,2,0,1:T(8,128)S(1)}, f32[4,1,2048,128]{3,2,0,1:T(8,128)}, u32[]{:S(2)}) copy-start(f32[4,1,2048,128]{3,2,0,1:T(8,128)} %get-tuple-element.63) | copy-start | bytes 12582916
  249.6 452.5 %reduce-scatter.15.cloned.1.call-start = ((), (), s32[]{:S(2)}) async-start(), calls=%async_computation.12 | async-start | bytes 2621440 | tf_op jit(solution)/shard_map/reduce_scatter | solution.py:236
  283.2 418.9 %reduce-scatter.13.cloned.1.call-start = ((), (), s32[]{:S(2)}) async-start(), calls=%async_computation.11 | async-start | bytes 2621440 | tf_op jit(solution)/shard_map/reduce_scatter | solution.py:236
  316.9 385.3 %reduce-scatter.11.cloned.1.call-start = ((), (), s32[]{:S(2)}) async-start(), calls=%async_computation.10 | async-start | bytes 2621440 | tf_op jit(solution)/shard_map/reduce_scatter | solution.py:236
  382.8 5.0 copy-start.8
  387.8 322.0 %reduce-scatter.9.cloned.1.call-start = ((), (), s32[]{:S(2)}) async-start(), calls=%async_computation.9 | async-start | bytes 5242880 | tf_op jit(solution)/shard_map/reduce_scatter | solution.py:236
  477.1 1.6 copy-start.9
  477.1 232.6 %reduce-scatter.7.cloned.1.call-start = ((), (), s32[]{:S(2)}) async-start(), calls=%async_computation.8 | async-start | bytes 5242880 | tf_op jit(solution)/shard_map/reduce_scatter | solution.py:236
  478.7 4.3 copy-start.7
  478.7 4.3 copy-start.10
  576.0 5.5 copy-start.6
  580.9 7.7 %collective-permute-start.7 = (f32[4,256,1024]{2,1,0:T(8,128)}, f32[4,256,1024]{2,1,0:T(8,128)}, u32[]{:S(2)}, u32[]{:S(2)}) collective-permute-start(f32[4,256,1024]{2,1,0:T(8,128)} %dynamic-slice_bitcast_fusion), channel_id=1, source_target_pairs={{0,4},{4,0},{8,12},{12,8},{16,20},{20,16},{24,28},{28,24},{1,5},{5... | collective-permute-start | bytes 12582920 | tf_op jit(solution)/shard_map/ppermute | solution.py:185
  593.1 2.0 copy-start
  593.1 3.5 copy-start.11
  593.1 3.5 copy-start.12
  595.2 48.6 %collective-permute-start.8 = (f32[2,256,1024]{2,1,0:T(8,128)S(1)}, f32[2,256,1024]{2,1,0:T(8,128)}, u32[]{:S(2)}, u32[]{:S(2)}) collective-permute-start(f32[2,256,1024]{2,1,0:T(8,128)S(1)} %dynamic-slice_bitcast_fusion.1), channel_id=1, source_target_pairs={{0,8},{4,12},{8,0},{12,4},{16,24},{20,28},{24,16},{28,20},{1,9},{5... | collective-permute-start | bytes 6291464 | tf_op jit(solution)/shard_map/ppermute | solution.py:185
  596.6 1.6 collective-permute-start.2
  598.3 50.6 %collective-permute-start.3 = (f32[256,256]{1,0:T(8,128)S(1)}, f32[256,256]{1,0:T(8,128)S(1)}, u32[]{:S(2)}, u32[]{:S(2)}) collective-permute-start(f32[256,256]{1,0:T(8,128)S(1)} %add.70), channel_id=1, source_target_pairs={{0,8},{4,12},{8,0},{12,4},{16,24},{20,28},{24,16},{28,20},{1,9},{5... | collective-permute-start | bytes 786440 | tf_op jit(solution)/shard_map/ppermute | solution.py:185
  647.5 59.2 %collective-permute-start.9 = (f32[1,256,1024]{2,1,0:T(8,128)}, f32[1,256,1024]{2,1,0:T(8,128)}, u32[]{:S(2)}, u32[]{:S(2)}) collective-permute-start(f32[1,256,1024]{2,1,0:T(8,128)} %constant_dynamic-slice_fusion), channel_id=1, source_target_pairs={{0,16},{4,20},{8,24},{12,28},{16,0},{20,4},{24,8},{28,12},{1,17},{... | collective-permute-start | bytes 3145736 | tf_op jit(solution)/shard_map/ppermute | solution.py:185
  648.9 28.6 %collective-permute-start.4 = (f32[256,256]{1,0:T(8,128)S(1)}, f32[256,256]{1,0:T(8,128)S(1)}, u32[]{:S(2)}, u32[]{:S(2)}) collective-permute-start(f32[256,256]{1,0:T(8,128)S(1)} %add.71), channel_id=1, source_target_pairs={{0,16},{4,20},{8,24},{12,28},{16,0},{20,4},{24,8},{28,12},{1,17},{... | collective-permute-start | bytes 786440 | tf_op jit(solution)/shard_map/ppermute | solution.py:185
  677.6 6.5 collective-permute-start.5
  684.1 12.1 %collective-permute-start.6 = (f32[256,256]{1,0:T(8,128)S(1)}, f32[256,256]{1,0:T(8,128)S(1)}, u32[]{:S(2)}, u32[]{:S(2)}) collective-permute-start(f32[256,256]{1,0:T(8,128)S(1)} %add.73), channel_id=1, source_target_pairs={{0,2},{1,3},{2,0},{3,1},{4,6},{5,7},{6,4},{7,5},{8,10},{9,11},{10,... | collective-permute-start | bytes 786440 | tf_op jit(solution)/shard_map/ppermute | solution.py:185
Sparse Core Ops, SparseCore 0:
  10.4 55.3 all-gather.4
  68.3 52.6 all-gather.2
  249.7 44.0 reduce-scatter.16
  296.0 43.1 reduce-scatter.14
  341.4 43.1 reduce-scatter.12
  387.9 43.9 reduce-scatter.10
  477.2 76.8 reduce-scatter.8
  586.1 76.6 reduce-scatter.6

commit v2 on v1

--- a/solution.py
+++ b/solution.py
@@ -187,30 +187,25 @@
 
 def gather_row(x):
     s, f, k = x.shape
-    n = lax.axis_size("row")
-    x = jnp.transpose(x, (1, 0, 2)).reshape(f * s, k)
-    groups = [list(range(c, n, 2)) for c in range(2)]
-    mine = lax.all_gather(x, "row", axis=0, axis_index_groups=groups)
-    other = swap(mine, "row", 1)
-    first_core = lax.rem(lax.axis_index("row"), 2) == 0
-    even = jnp.where(first_core, mine, other)
-    odd = jnp.where(first_core, other, mine)
-    return jnp.transpose(jnp.stack([even, odd], 1), (2, 0, 1, 3)).reshape(f * s, n * k)
-
-
-def sum_to_row(x):
+    whole_bond = lax.all_gather(jnp.transpose(x, (1, 0, 2)), "row", axis=2, tiled=True)
+    return whole_bond.reshape(f * s, -1)
+
+
+def sum_to_row(x, high_first):
     n = lax.axis_size("row")
     me = lax.axis_index("row")
-    x = x.reshape((n, -1) + x.shape[1:])
-    bit = 1
-    while bit < n:
-        x = x.reshape((x.shape[0] // 2, 2) + x.shape[1:])
-        mine = lax.rem(me // bit, 2)
-        keep = lax.dynamic_index_in_dim(x, mine, 1, keepdims=False)
-        send = lax.dynamic_index_in_dim(x, 1 - mine, 1, keepdims=False)
-        x = keep + swap(send, "row", bit)
-        bit *= 2
-    return x[0]
+    count = n.bit_length() - 1
+    left = list(range(count))[::-1]
+    order = [0] + (left[:-1] if high_first else left[:-1][::-1])
+    x = x.reshape((2,) * count + (x.shape[0] // n,) + x.shape[1:])
+    for b in order:
+        axis = left.index(b)
+        left.remove(b)
+        mine = lax.rem(me // 2**b, 2)
+        keep = lax.dynamic_index_in_dim(x, mine, axis, keepdims=False)
+        send = lax.dynamic_index_in_dim(x, 1 - mine, axis, keepdims=False)
+        x = keep + swap(send, "row", 2**b)
+    return x
 
 
 def sum_all(x):
@@ -251,7 +246,9 @@
         edges.append(scatter(edge_terms))
         rights.append(right_terms)
         sites.append(site_terms)
-    right_sum = sum_to_row(sum(rights))
+    total = sum(rights)
+    half = chi // 2
+    right_sum = jnp.concatenate([sum_to_row(total[:, :half], True), sum_to_row(total[:, half:], False)], 1)
     right_gradient = jnp.transpose(right_sum.reshape(-1, s, chi), (1, 0, 2))
     site_gradient = jnp.transpose(sum_all(sum(sites)).reshape(d, d, d, d), (1, 3, 2, 0))
     return jnp.concatenate(edges, 0), site_gradient, jnp.concatenate(lefts, 0), right_gradient

time: 731 us -> 609 us (0.83)
  local copies, waits for them, and re-layouts: 157 us -> 104 us
  waiting for transfers between devices: 200 us -> 147 us
  other arithmetic: 66 us -> 50.5 us
    ppermute x10 -> x11, waiting for transfers between devices: 91.3 us -> 54 us  [swap(): return lax.ppermute(x, axis, [(i, i ^ bit) for i in range(n)])]
    transpose x2 -> x0, local copies, waits for them, and re-layouts: 33 us -> none  [gather_row(): jnp.transpose(jnp.stack([even, odd], 1), (2, 0, 1, 3)).reshape(f * s, n * k)]
    reshape x2 -> x0, local copies, waits for them, and re-layouts: 23.4 us -> none  [gather_row(): jnp.transpose(jnp.stack([even, odd], 1), (2, 0, 1, 3)).reshape(f * s, n * k)]
    all_gather x0 -> x2, local copies, waits for them, and re-layouts: none -> 16.7 us  [gather_row(): lax.all_gather(jnp.transpose(x, (1, 0, 2)), 'row', axis=2, tiled=True)]
    all_gather x2, waiting for transfers between devices: 108 us -> 91.9 us  [gather_row(): lax.all_gather(jnp.transpose(x, (1, 0, 2)), 'row', axis=2, tiled=True)]
    transpose x1, local copies, waits for them, and re-layouts: 12.2 us -> 2.11 us  [with_kernels(): jnp.transpose(site_tensor, (2, 1, 3, 0)).reshape(d * d, d * d)]
    unnamed x31 -> x23, local copies, waits for them, and re-layouts: 16.3 us -> 10.1 us
    concatenate x4 -> x2, other arithmetic: 16 us -> 11.8 us  [with_kernels(): first = tuple((jnp.concatenate([p[k] for p in part], 0) for k in range(2)))]
  transfers between devices with their start and end apart: 18 -> 19, of which waited for: 9 -> 7; matrix products, arithmetic and copies ran while one was open for 18% -> 22% of each run, Pallas kernels for 34% -> 41%
where the time goes in v2:
time: 609 us; the launch traced here: 599 us
  Pallas kernels  274 us (45%)
  waiting for transfers between devices  147 us (24%)
  local copies, waits for them, and re-layouts  104 us (17%)
  other arithmetic  50.5 us (8%)
  between operations  14.8 us (2%)
  starting transfers between devices  8.44 us (1%)
    pallas_call x2, Pallas kernels, backward(): pl.pallas_call(functools.partial(backward_kernel, d, s), grid=(rows // BL...  156 us
    pallas_call x4, Pallas kernels, forward(): pl.pallas_call(functools.partial(forward_kernel, d, s), grid=(rows // BLO...  118 us
    all_gather x2, waiting for transfers between devices, gather_row(): lax.all_gather(jnp.transpose(x, (1, 0, 2)), 'row', axis=2, tiled=True)  91.9 us
    ppermute x11, waiting for transfers between devices, swap(): return lax.ppermute(x, axis, [(i, i ^ bit) for i in range(n)])  54 us
    reshape x6, local copies, waits for them, and re-layouts, scatter(): terms.reshape(-1, d, chi)  30.3 us
    all_gather x2, local copies, waits for them, and re-layouts, gather_row(): lax.all_gather(jnp.transpose(x, (1, 0, 2)), 'row', axis=2, tiled=True)  16.7 us
  transfers between devices with their start and end apart: 19, of which 7 were waited for; matrix products, arithmetic and copies ran while one was open for 22% of the time, Pallas kernels for 41%

profile of v2, /device:TPU:0, one launch (start us, length us, event | category | flops | bytes accessed | tf_op | source)
XLA Modules:
  0.0 598.9 jit_solution(15137891046141971690)
XLA Ops:
  8.7 3.1 copy.20
  13.5 7.5 %fusion.5 = (f32[32,16,1024]{2,1,0:T(8,128)}, f32[32,16,1024]{2,1,0:T(8,128)}, f32[32,16,1024]{2,1,0:T(8,128)}, f32[32,16,1024]{2,1,0:T(8,128)}) fusion(f32[128,16,1024]{2,1,0:T(8,128)} %param.5), kind=kLoop, calls=%fused_computation.32 | loop fusion | bytes 16777216 | tf_op jit(solution)/shard_map/split | solution.py:236
  21.0 47.5 %all-gather.3.cloned.1.call-done = f32[16,128,1024]{2,0,1:T(8,128)} async-done(((f32[16,128,128]{2,0,1:T(8,128)}), f32[16,128,1024]{2,0,1:T(8,128)}) %all-gather.3.cloned.1.call-update) | async-done | bytes 8388624 | tf_op jit(solution)/shard_map/all_gather | solution.py:190
  68.6 8.2 %copy.21 = f32[16,128,1024]{2,1,0:T(8,128)S(1)} copy(f32[16,128,1024]{2,0,1:T(8,128)} %all-gather.3.cloned.1.call-done) | data formatting | bytes 16777216 | tf_op jit(solution)/shard_map/all_gather | solution.py:190
  76.8 5.3 fusion
  82.1 44.4 %all-gather.5.cloned.1.call-done = f32[16,128,1024]{2,0,1:T(8,128)} async-done(((f32[16,128,128]{2,0,1:T(8,128)}), f32[16,128,1024]{2,0,1:T(8,128)}) %all-gather.5.cloned.1.call-update) | async-done | bytes 8388624 | tf_op jit(solution)/shard_map/all_gather | solution.py:190
  126.4 8.4 %copy.22 = f32[16,128,1024]{2,1,0:T(8,128)S(1)} copy(f32[16,128,1024]{2,0,1:T(8,128)} %all-gather.5.cloned.1.call-done) | data formatting | bytes 16777216 | tf_op jit(solution)/shard_map/all_gather | solution.py:190
  134.9 5.1 fusion.1
  140.0 29.2 %forward.7 = (f32[512,1024]{1,0:T(8,128)}, bf16[512,2048]{1,0:T(8,128)(2,1)}, bf16[512,2048]{1,0:T(8,128)(2,1)}) custom-call(f32[512,1024]{1,0:T(8,128)} %bitcast.79, bf16[256,256]{1,0:T(8,128)(2,1)} %get-tuple-element.65.sh_ref, bf16[256,256]{1,0:T(8,128)(2,1)} %get-tuple-element.64.sl_ref, bf16[2048,1024]{1,0:T(8,128)(2,1)} %get-tuple-element.61.rh_ref, ...), custom_call_target="tpu_custom_call" | custom-call | flops 12884901888 | bytes 20971520 | tf_op jit(solution)/shard_map/forward/pallas_call | solution.py:142
  169.2 4.2 copy.30
  173.5 29.4 %forward.6 = (f32[512,1024]{1,0:T(8,128)}, bf16[512,2048]{1,0:T(8,128)(2,1)}, bf16[512,2048]{1,0:T(8,128)(2,1)}) custom-call(f32[512,1024]{1,0:T(8,128)} %bitcast.78, bf16[256,256]{1,0:T(8,128)(2,1)} %get-tuple-element.65.sh_ref, bf16[256,256]{1,0:T(8,128)(2,1)} %get-tuple-element.64.sl_ref, bf16[2048,1024]{1,0:T(8,128)(2,1)} %get-tuple-element.61.rh_ref, ...), custom_call_target="tpu_custom_call" | custom-call | flops 12884901888 | bytes 20971520 | tf_op jit(solution)/shard_map/forward/pallas_call | solution.py:142
  202.9 4.2 copy.29
  207.2 29.8 %forward.5 = (f32[512,1024]{1,0:T(8,128)}, bf16[512,2048]{1,0:T(8,128)(2,1)}, bf16[512,2048]{1,0:T(8,128)(2,1)}) custom-call(f32[512,1024]{1,0:T(8,128)} %bitcast.77, bf16[256,256]{1,0:T(8,128)(2,1)} %get-tuple-element.65.sh_ref, bf16[256,256]{1,0:T(8,128)(2,1)} %get-tuple-element.64.sl_ref, bf16[2048,1024]{1,0:T(8,128)(2,1)} %get-tuple-element.61.rh_ref, ...), custom_call_target="tpu_custom_call" | custom-call | flops 12884901888 | bytes 20971520 | tf_op jit(solution)/shard_map/forward/pallas_call | solution.py:142
  237.0 4.4 copy.28
  246.7 8.5 %fusion.7 = (f32[64,16,1024]{2,1,0:T(8,128)}, f32[64,16,1024]{2,1,0:T(8,128)}) fusion(f32[128,16,1024]{2,1,0:T(8,128)} %param.5), kind=kLoop, calls=%fused_computation.34 | loop fusion | bytes 16777216 | tf_op jit(solution)/shard_map/split | solution.py:242
  255.2 8.5 %fusion.6 = (f32[64,16,1024]{2,1,0:T(8,128)}, f32[64,16,1024]{2,1,0:T(8,128)}) fusion(f32[128,16,1024]{2,1,0:T(8,128)} %param.7), kind=kLoop, calls=%fused_computation.33 | loop fusion | bytes 16777216 | tf_op jit(solution)/shard_map/split | solution.py:242
  263.7 29.2 %forward.4 = (f32[512,1024]{1,0:T(8,128)}, bf16[512,2048]{1,0:T(8,128)(2,1)}, bf16[512,2048]{1,0:T(8,128)(2,1)}) custom-call(f32[512,1024]{1,0:T(8,128)} %bitcast.76, bf16[256,256]{1,0:T(8,128)(2,1)} %get-tuple-element.65.sh_ref, bf16[256,256]{1,0:T(8,128)(2,1)} %get-tuple-element.64.sl_ref, bf16[2048,1024]{1,0:T(8,128)(2,1)} %get-tuple-element.61.rh_ref, ...), custom_call_target="tpu_custom_call" | custom-call | flops 12884901888 | bytes 20971520 | tf_op jit(solution)/shard_map/forward/pallas_call | solution.py:142
  292.9 4.3 copy.27
  297.3 5.9 pad_maximum_fusion.2
  303.2 78.1 %backward.3 = (f32[1024,1024]{1,0:T(8,128)}, f32[2048,1024]{1,0:T(8,128)}, f32[256,256]{1,0:T(8,128)}) custom-call(f32[1024,1024]{1,0:T(8,128)} %bitcast.69, f32[1024,1024]{1,0:T(8,128)} %bitcast.70, bf16[1024,2048]{1,0:T(8,128)(2,1)} %get-tuple-element.66.fh_ref, bf16[1024,2048]{1,0:T(8,128)(2,1)} %get-tuple-element.67.fl_ref, ...), custom_call_target="tpu_custom_call" | custom-call | flops 42949672960 | bytes 25165824 | tf_op jit(solution)/shard_map/backward/pallas_call | solution.py:164
  381.4 6.6 %copy.25 = f32[64,16,1024]{2,0,1:T(8,128)} copy(f32[64,16,1024]{2,1,0:T(8,128)} %bitcast.65) | data formatting | bytes 8388608 | tf_op jit(solution)/shard_map/reshape | solution.py:231
  389.6 5.9 pad_maximum_fusion
  395.5 78.1 %backward.2 = (f32[1024,1024]{1,0:T(8,128)}, f32[2048,1024]{1,0:T(8,128)}, f32[256,256]{1,0:T(8,128)}) custom-call(f32[1024,1024]{1,0:T(8,128)} %bitcast.67, f32[1024,1024]{1,0:T(8,128)} %bitcast.68, bf16[1024,2048]{1,0:T(8,128)(2,1)} %get-tuple-element.68.fh_ref, bf16[1024,2048]{1,0:T(8,128)(2,1)} %get-tuple-element.69.fl_ref, ...), custom_call_target="tpu_custom_call" | custom-call | flops 42949672960 | bytes 25165824 | tf_op jit(solution)/shard_map/backward/pallas_call | solution.py:164
  473.6 6.6 %copy.24 = f32[64,16,1024]{2,0,1:T(8,128)} copy(f32[64,16,1024]{2,1,0:T(8,128)} %bitcast.64) | data formatting | bytes 8388608 | tf_op jit(solution)/shard_map/reshape | solution.py:231
  480.2 12.0 %add.91 = f32[2048,1024]{1,0:T(8,128)} add(f32[2048,1024]{1,0:T(8,128)} %get-tuple-element.38, f32[2048,1024]{1,0:T(8,128)} %get-tuple-element.39) | non-fusion elementwise | flops 2097152 | bytes 25165824 | tf_op jit(solution)/shard_map/add | solution.py:249
  492.2 4.4 fusion.4
  511.1 25.0 %collective-permute-done.1 = f32[256,256]{1,0:T(8,128)S(1)} collective-permute-done((f32[256,256]{1,0:T(8,128)S(1)}, f32[256,256]{1,0:T(8,128)S(1)}, u32[]{:S(2)}, u32[]{:S(2)}) %collective-permute-start.1) | collective-permute-done | bytes 262176 | tf_op jit(solution)/shard_map/ppermute | solution.py:185
  536.6 7.4 %collective-permute-done.2 = f32[256,256]{1,0:T(8,128)} collective-permute-done((f32[256,256]{1,0:T(8,128)S(1)}, f32[256,256]{1,0:T(8,128)}, u32[]{:S(2)}, u32[]{:S(2)}) %collective-permute-start.2) | collective-permute-done | bytes 262176 | tf_op jit(solution)/shard_map/ppermute | solution.py:185
  553.7 7.7 %collective-permute-done.3 = f32[256,256]{1,0:T(8,128)S(1)} collective-permute-done((f32[256,256]{1,0:T(8,128)S(1)}, f32[256,256]{1,0:T(8,128)S(1)}, u32[]{:S(2)}, u32[]{:S(2)}) %collective-permute-start.3) | collective-permute-done | bytes 262176 | tf_op jit(solution)/shard_map/ppermute | solution.py:185
  561.7 13.3 %collective-permute-done.4 = f32[256,256]{1,0:T(8,128)S(1)} collective-permute-done((f32[256,256]{1,0:T(8,128)S(1)}, f32[256,256]{1,0:T(8,128)S(1)}, u32[]{:S(2)}, u32[]{:S(2)}) %collective-permute-start.4) | collective-permute-done | bytes 262176 | tf_op jit(solution)/shard_map/ppermute | solution.py:185
  575.6 2.8 copy.26
  584.5 2.7 copy.32
  (89 shorter events, 46.1 us)
Async XLA Ops:
  7.2 61.4 %all-gather.3.cloned.1.call-start = ((), (), s32[]{:S(2)}) async-start(), calls=%async_computation.6 | async-start | bytes 9437184 | tf_op jit(solution)/shard_map/all_gather | solution.py:190
  7.9 118.5 %all-gather.5.cloned.1.call-start = ((), (), s32[]{:S(2)}) async-start(), calls=%async_computation.7 | async-start | bytes 9437184 | tf_op jit(solution)/shard_map/all_gather | solution.py:190
  8.6 574.1 %reduce-scatter.17.cloned.1.call-start = ((), (), s32[]{:S(2)}) async-start(), calls=%async_computation.13 | async-start | bytes 2621440 | tf_op jit(solution)/shard_map/reduce_scatter | solution.py:231
  173.4 409.3 %reduce-scatter.15.cloned.1.call-start = ((), (), s32[]{:S(2)}) async-start(), calls=%async_computation.12 | async-start | bytes 2621440 | tf_op jit(solution)/shard_map/reduce_scatter | solution.py:231
  207.1 375.7 %reduce-scatter.13.cloned.1.call-start = ((), (), s32[]{:S(2)}) async-start(), calls=%async_computation.11 | async-start | bytes 2621440 | tf_op jit(solution)/shard_map/reduce_scatter | solution.py:231
  236.9 4.4 copy-start.4
  241.3 341.4 %reduce-scatter.11.cloned.1.call-start = ((), (), s32[]{:S(2)}) async-start(), calls=%async_computation.10 | async-start | bytes 2621440 | tf_op jit(solution)/shard_map/reduce_scatter | solution.py:231
  292.9 4.4 copy-start.6
  297.3 290.0 %reduce-scatter.9.cloned.1.call-start = ((), (), s32[]{:S(2)}) async-start(), calls=%async_computation.9 | async-start | bytes 5242880 | tf_op jit(solution)/shard_map/reduce_scatter | solution.py:231
  388.0 1.6 copy-start.7
  388.0 199.2 %reduce-scatter.7.cloned.1.call-start = ((), (), s32[]{:S(2)}) async-start(), calls=%async_computation.8 | async-start | bytes 5242880 | tf_op jit(solution)/shard_map/reduce_scatter | solution.py:231
  496.7 3.3 copy-start
  496.7 4.7 copy-start.2
  496.7 4.9 copy-start.8
  496.7 4.9 copy-start.9
  498.2 4.4 collective-permute-start.8
  501.3 5.2 collective-permute-start.5
  501.6 4.9 copy-start.1
  501.6 8.8 %collective-permute-start = (f32[256,256]{1,0:T(8,128)S(1)}, f32[256,256]{1,0:T(8,128)S(1)}, u32[]{:S(2)}, u32[]{:S(2)}) collective-permute-start(f32[256,256]{1,0:T(8,128)S(1)} %add.85), channel_id=1, source_target_pairs={{0,4},{4,0},{8,12},{12,8},{16,20},{20,16},{24,28},{28,24},{1,5},{5... | collective-permute-start | bytes 786440 | tf_op jit(solution)/shard_map/ppermute | solution.py:185
  505.0 3.7 copy-start.3
  505.1 41.4 %collective-permute-start.9 = (f32[2,256,512]{2,1,0:T(8,128)S(1)}, f32[2,256,512]{2,1,0:T(8,128)}, u32[]{:S(2)}, u32[]{:S(2)}) collective-permute-start(f32[2,256,512]{2,1,0:T(8,128)S(1)} %dynamic-slice_bitcast_fusion.2), channel_id=1, source_target_pairs={{0,8},{4,12},{8,0},{12,4},{16,24},{20,28},{24,16},{28,20},{1,9},{5... | collective-permute-start | bytes 3145736 | tf_op jit(solution)/shard_map/ppermute | solution.py:185
  509.7 40.2 %collective-permute-start.6 = (f32[2,256,512]{2,1,0:T(8,128)}, f32[2,256,512]{2,1,0:T(8,128)}, u32[]{:S(2)}, u32[]{:S(2)}) collective-permute-start(f32[2,256,512]{2,1,0:T(8,128)} %dynamic-slice_bitcast_fusion.3), channel_id=1, source_target_pairs={{0,16},{4,20},{8,24},{12,28},{16,0},{20,4},{24,8},{28,12},{1,17},{... | collective-permute-start | bytes 3145736 | tf_op jit(solution)/shard_map/ppermute | solution.py:185
  510.5 25.6 %collective-permute-start.1 = (f32[256,256]{1,0:T(8,128)S(1)}, f32[256,256]{1,0:T(8,128)S(1)}, u32[]{:S(2)}, u32[]{:S(2)}) collective-permute-start(f32[256,256]{1,0:T(8,128)S(1)} %add.86), channel_id=1, source_target_pairs={{0,8},{4,12},{8,0},{12,4},{16,24},{20,28},{24,16},{28,20},{1,9},{5... | collective-permute-start | bytes 786440 | tf_op jit(solution)/shard_map/ppermute | solution.py:185
  536.1 7.9 %collective-permute-start.2 = (f32[256,256]{1,0:T(8,128)S(1)}, f32[256,256]{1,0:T(8,128)}, u32[]{:S(2)}, u32[]{:S(2)}) collective-permute-start(f32[256,256]{1,0:T(8,128)S(1)} %add.87), channel_id=1, source_target_pairs={{0,16},{4,20},{8,24},{12,28},{16,0},{20,4},{24,8},{28,12},{1,17},{... | collective-permute-start | bytes 786440 | tf_op jit(solution)/shard_map/ppermute | solution.py:185
  545.0 16.4 %collective-permute-start.3 = (f32[256,256]{1,0:T(8,128)S(1)}, f32[256,256]{1,0:T(8,128)S(1)}, u32[]{:S(2)}, u32[]{:S(2)}) collective-permute-start(f32[256,256]{1,0:T(8,128)S(1)} %add.88), channel_id=1, source_target_pairs={{0,1},{1,0},{2,3},{3,2},{4,5},{5,4},{6,7},{7,6},{8,9},{9,8},{10,11... | collective-permute-start | bytes 786440 | tf_op jit(solution)/shard_map/ppermute | solution.py:185
  549.1 29.4 %collective-permute-start.10 = (f32[256,512]{1,0:T(8,128)}, f32[256,512]{1,0:T(8,128)}, u32[]{:S(2)}, u32[]{:S(2)}) collective-permute-start(f32[256,512]{1,0:T(8,128)} %dynamic-slice_bitcast_fusion.4), channel_id=1, source_target_pairs={{0,16},{4,20},{8,24},{12,28},{16,0},{20,4},{24,8},{28,12},{1,17},{... | collective-permute-start | bytes 1572872 | tf_op jit(solution)/shard_map/ppermute | solution.py:185
  551.3 23.6 %copy-start.5 = (f32[2,256,512]{2,1,0:T(8,128)}, f32[2,256,512]{2,1,0:T(8,128)S(1)}, u32[]{:S(2)}) copy-start(f32[2,256,512]{2,1,0:T(8,128)S(1)} %bitcast_add_fusion.3) | copy-start | bytes 3145732
  552.3 27.3 %collective-permute-start.7 = (f32[256,512]{1,0:T(8,128)}, f32[256,512]{1,0:T(8,128)}, u32[]{:S(2)}, u32[]{:S(2)}) collective-permute-start(f32[256,512]{1,0:T(8,128)} %dynamic-slice_bitcast_fusion.5), channel_id=1, source_target_pairs={{0,8},{4,12},{8,0},{12,4},{16,24},{20,28},{24,16},{28,20},{1,9},{5... | collective-permute-start | bytes 1572872 | tf_op jit(solution)/shard_map/ppermute | solution.py:185
  561.4 13.5 %collective-permute-start.4 = (f32[256,256]{1,0:T(8,128)S(1)}, f32[256,256]{1,0:T(8,128)S(1)}, u32[]{:S(2)}, u32[]{:S(2)}) collective-permute-start(f32[256,256]{1,0:T(8,128)S(1)} %add.89), channel_id=1, source_target_pairs={{0,2},{1,3},{2,0},{3,1},{4,6},{5,7},{6,4},{7,5},{8,10},{9,11},{10,... | collective-permute-start | bytes 786440 | tf_op jit(solution)/shard_map/ppermute | solution.py:185
Sparse Core Ops, SparseCore 0:
  9.9 58.6 all-gather.2
  70.4 55.9 all-gather.4
  173.6 43.8 reduce-scatter.16
  219.7 43.1 reduce-scatter.14
  265.1 43.1 reduce-scatter.12
  311.1 43.1 reduce-scatter.10
  388.2 76.6 reduce-scatter.8
  480.3 82.1 reduce-scatter.6
